TPU v7x, 32 devices: a whole 2x2x4 slice. The times are simulated.
32 devices in a mesh: seq: 8 (over z, core), tensor: 4 (over y, x).
Axes of the slice: x: 2, y: 2, z: 4, core: 2. Of those that a mesh axis runs over, the one named last changes fastest.
Arguments:
- queries: bfloat16 [6144, 4096], P('seq', 'tensor'), may hold values from -12 to 12
- keys: bfloat16 [6144, 1024], P('seq', 'tensor'), may hold values from -12 to 12
- values: bfloat16 [6144, 1024], P('seq', 'tensor'), may hold values from -6 to 6
- out_weight: bfloat16 [4096, 4096], P('tensor'), may hold values from -0.09375 to 0.09375
- out_grad: bfloat16 [6144, 4096], P('seq', 'tensor'), may hold values from -6 to 6
- doc_ids: int32 [6144], P('seq'), may hold values from 0 to 3, never falling along the last dimension, each value on 1 to 3072 neighbouring positions
Outputs:
- grad_queries: bfloat16 [6144, 4096], P('seq', 'tensor')
- grad_keys: bfloat16 [6144, 1024], P('seq', 'tensor')
- grad_values: bfloat16 [6144, 1024], P('seq', 'tensor')
- grad_out_weight: bfloat16 [4096, 4096], P('tensor', 'seq')
Inputs may be any that keep to these rules, and one draw needn't show every extreme that they name: `doc_ids`: document numbers never fall along the sequence; a document holds 1 to 3072 tokens and one holds exactly that many.
All inputs are finite; a program needn't handle non-finite values.
Results may differ from a plain program's by a relative error of at most 0.015.
Values may be sent and summed in bfloat16 or wider, within the bound.
A program may use at most 192 MiB of HBM per device.

v0:
```python
import math

import jax
import jax.numpy as jnp
from jax import lax
from jax.sharding import PartitionSpec as P

HEAD_SIZE = 128


NEG_BIG = -1e30


def shifted(value, axis, steps):
    count = lax.axis_size(axis)
    initial, last = (max(0, -steps), min(count, count - steps))
    return lax.ppermute(value, axis, [(source, source + steps) for source in range(initial, last)])


def contract_rows(left, right):
    return lax.dot_general(
        left, right, (((0,), (0,)), ((), ())), preferred_element_type=jnp.float32
    )


def contract_last(left, right):
    return lax.dot_general(
        left, right, (((1,), (1,)), ((), ())), preferred_element_type=jnp.float32
    )


def head_probs(q_head, k_group, visible, scale):
    raw = contract_last(q_head, k_group) * scale
    masked = jnp.where(visible, raw, NEG_BIG)
    top = jnp.max(masked, axis=1, keepdims=True)
    expo = jnp.where(visible, jnp.exp(masked - top), 0.0)
    return expo / jnp.sum(expo, axis=1, keepdims=True)


def head_grads(q_head, k_group, v_group, probs, attn_head, grad_head, scale):
    probs_low = probs.astype(jnp.bfloat16)
    delta = jnp.sum(
        grad_head.astype(jnp.float32) * attn_head.astype(jnp.float32), axis=1, keepdims=True
    )
    d_prob = contract_last(grad_head, v_group)
    d_score = (probs * (d_prob - delta)).astype(jnp.bfloat16)
    query_gradient = jnp.dot(d_score, k_group, preferred_element_type=jnp.float32) * scale
    key_gradient = contract_rows(d_score, q_head) * scale
    value_gradient = contract_rows(probs_low, grad_head)
    return (query_gradient, key_gradient, value_gradient)


def local(queries, keys, values, out_weight, out_grad, doc_ids):
    tok = queries.shape[0]
    q_heads = queries.shape[1] // HEAD_SIZE
    kv_heads = keys.shape[1] // HEAD_SIZE
    group_factor = q_heads // kv_heads
    scale = 1.0 / math.sqrt(HEAD_SIZE)
    shard = lax.axis_index("seq")
    fetched = []
    for hop in (2, 1):
        fetched.append(shifted((keys, values, doc_ids), "seq", hop))
    distant_part, nearby_part = fetched
    key_all = jnp.concatenate([distant_part[0], nearby_part[0], keys], axis=0)
    value_all = jnp.concatenate([distant_part[1], nearby_part[1], values], axis=0)
    doc_keys = jnp.concatenate([distant_part[2], nearby_part[2], doc_ids])
    q_pos = shard * tok + jnp.arange(tok, dtype=jnp.int32)
    k_pos = (shard - 2) * tok + jnp.arange(3 * tok, dtype=jnp.int32)
    gap = q_pos[:, None] - k_pos[None, :]
    visible = (
        (gap >= 0)
        & (gap < 2 * tok)
        & (k_pos[None, :] >= 0)
        & (doc_ids[:, None] == doc_keys[None, :])
    )
    grad_full = lax.all_gather(out_grad, "tensor", axis=1, tiled=True)
    attention_gradient = contract_last(grad_full, out_weight).astype(jnp.bfloat16)
    grad_q_list = []
    grad_k_list = [jnp.zeros((3 * tok, HEAD_SIZE), jnp.float32) for index in range(kv_heads)]
    grad_v_list = [jnp.zeros((3 * tok, HEAD_SIZE), jnp.float32) for index in range(kv_heads)]
    attn_list = []
    for head in range(q_heads):
        kv_index = head // group_factor
        q_head = queries[:, head * HEAD_SIZE : (head + 1) * HEAD_SIZE]
        k_group = key_all[:, kv_index * HEAD_SIZE : (kv_index + 1) * HEAD_SIZE]
        v_group = value_all[:, kv_index * HEAD_SIZE : (kv_index + 1) * HEAD_SIZE]
        grad_head = attention_gradient[:, head * HEAD_SIZE : (head + 1) * HEAD_SIZE]
        probs = head_probs(q_head, k_group, visible, scale)
        attn_head = jnp.dot(
            probs.astype(jnp.bfloat16), v_group, preferred_element_type=jnp.float32
        ).astype(jnp.bfloat16)
        attn_list.append(attn_head)
        query_gradient, key_gradient, value_gradient = head_grads(
            q_head, k_group, v_group, probs, attn_head, grad_head, scale
        )
        grad_q_list.append(query_gradient)
        grad_k_list[kv_index] = grad_k_list[kv_index] + key_gradient
        grad_v_list[kv_index] = grad_v_list[kv_index] + value_gradient
    attn_all = jnp.concatenate(attn_list, axis=1)
    summed = lax.psum_scatter(
        contract_rows(grad_full, attn_all), "seq", scatter_dimension=0, tiled=True
    )
    weight_grad = summed.T.astype(jnp.bfloat16)
    key_blocks = jnp.concatenate(grad_k_list, axis=1)
    value_blocks = jnp.concatenate(grad_v_list, axis=1)
    total_k = key_blocks[2 * tok :]
    total_v = value_blocks[2 * tok :]
    for hop in (1, 2):
        begin = (2 - hop) * tok
        returned = shifted(
            (key_blocks[begin : begin + tok], value_blocks[begin : begin + tok]), "seq", -hop
        )
        total_k = total_k + returned[0]
        total_v = total_v + returned[1]
    grad_queries = jnp.concatenate(grad_q_list, axis=1).astype(jnp.bfloat16)
    return (grad_queries, total_k.astype(jnp.bfloat16), total_v.astype(jnp.bfloat16), weight_grad)


def solution(mesh):
    placed = (
        P("seq", "tensor"),
        P("seq", "tensor"),
        P("seq", "tensor"),
        P("tensor", None),
        P("seq", "tensor"),
        P("seq"),
    )
    return jax.shard_map(
        local,
        mesh=mesh,
        in_specs=placed,
        out_specs=(P("seq", "tensor"), P("seq", "tensor"), P("seq", "tensor"), P("tensor", "seq")),
        check_vma=False,
    )
```

profile of v0, /device:TPU:0, one launch (start us, length us, event | category | flops | bytes accessed | tf_op | source)
XLA Modules:
  0.0 408.0 jit_solution(8071699774110517190)
XLA Ops:
  47.7 7.0 %fusion.10 = (f32[768]{0:T(1024)S(1)}, f32[768]{0:T(1024)S(1)}, f32[2304,768]{1,0:T(8,128)}) fusion(s32[2304]{0:T(1024)S(1)} %pad_add_fusion, s32[768]{0:T(1024)S(1)} %copy-done.12, pred[2304]{0:T(1024)(128)(4,1)S(1)} %broadcast_compare_fusion, s32[2304]{0:T(1024)S(1)} %iota_add_fusion, s32[768]{0:T(1024)S(1)} %iota_add_fusion.1, ...), kind=kOutput, calls=%fused_computation.37 | convolution fusion | flops 475986432 | bytes 14984192 | tf_op jit(solution)/shard_map/dot_general | solution.py:27
  54.8 21.0 %fusion.26 = (f32[768]{0:T(1024)S(1)}, f32[768]{0:T(1024)S(1)}, f32[768]{0:T(1024)S(1)}, f32[768]{0:T(1024)S(1)}, f32[768]{0:T(1024)S(1)}, /*index=5*/f32[768]{0...) fusion(f32[2304,768]{1,0:T(8,128)} %get-tuple-element.36, f32[768]{0:T(1024)S(1)} %get-tuple-element.24, ...), kind=kOutput, calls=%fused_computation.53 | convolution fusion | flops 514910208 | bytes 57478144 | tf_op jit(solution)/shard_map/dot_general | solution.py:27
  75.9 8.1 %constant_dynamic-update-slice_fusion.13 = (bf16[768,1024]{1,0:T(8,128)(2,1)S(1)}, bf16[768,128]{1,0:T(8,128)(2,1)}) fusion(bf16[2304,256]{1,0:T(8,128)(2,1)} %constant_dynamic-update-slice_fusion.3, f32[768]{0:T(1024)S(1)} %get-tuple-element.17, f32[768]{0:T(1024)S(1)} %get-tuple-element.25, f32[2304,768]{1,0:T(8,128)} %copy-done.4, ...), kind=kOutput, calls=%fused_computation.243 | convolution fusion | flops 476086272 | bytes 8093952 | tf_op jit(solution)/shard_map/dot_general | solution.py:89
  84.0 16.0 %fusion.24 = (f32[768]{0:T(1024)S(1)}, f32[768]{0:T(1024)S(1)}, f32[768]{0:T(1024)S(1)}, f32[768]{0:T(1024)S(1)}, f32[768]{0:T(1024)S(1)}, /*index=5*/f32[768]{0:T(1024)S(1)}) fusion(f32[2304,768]{1,0:T(8,128)S(1)} %fusion.109, f32[768]{0:T(1024)S(1)} %get-tuple-element.23, s32[2304]{0:T(1024)S(1)} %pad_add_fusion, s32[768]{0:T(1024)S(1)} %copy-done.12, ...), kind=kLoop, calls=%fused_computation.51 | loop fusion | flops 65465856 | bytes 42531072 | tf_op jit(solution)/shard_map/reduce_sum | solution.py:37
  100.1 6.1 %constant_dynamic-update-slice_fusion.12 = (bf16[768,1024]{1,0:T(8,128)(2,1)S(1)}, bf16[768,128]{1,0:T(8,128)(2,1)S(1)}) fusion(bf16[768,1024]{1,0:T(8,128)(2,1)S(1)} %get-tuple-element.39, bf16[2304,256]{1,0:T(8,128)(2,1)} %constant_dynamic-update-slice_fusion.3, f32[768]{0:T(1024)S(1)} %get-tuple-element.27, f32[768]{0:T(1024)S(1)} %get-tuple-element.18, ...), kind=kOutput, calls=%fused_computation.242 | convolution fusion | flops 476086272 | bytes 8104960 | tf_op jit(solution)/shard_map/dot_general | solution.py:89
  106.3 6.2 %constant_dynamic-update-slice_fusion.11 = (bf16[768,1024]{1,0:T(8,128)(2,1)S(1)}, bf16[768,128]{1,0:T(8,128)(2,1)S(1)}) fusion(bf16[768,1024]{1,0:T(8,128)(2,1)S(1)} %get-tuple-element.41, bf16[2304,256]{1,0:T(8,128)(2,1)} %constant_dynamic-update-slice_fusion.3, f32[768]{0:T(1024)S(1)} %get-tuple-element.28, f32[768]{0:T(1024)S(1)} %get-tuple-element.19, ...), kind=kOutput, calls=%fused_computation.241 | convolution fusion | flops 476086272 | bytes 8104960 | tf_op jit(solution)/shard_map/dot_general | solution.py:89
  112.6 7.2 %constant_dynamic-update-slice_fusion.10 = (bf16[768,1024]{1,0:T(8,128)(2,1)S(1)}, bf16[768,128]{1,0:T(8,128)(2,1)}) fusion(bf16[768,1024]{1,0:T(8,128)(2,1)S(1)} %get-tuple-element.43, bf16[2304,256]{1,0:T(8,128)(2,1)} %constant_dynamic-update-slice_fusion.3, f32[768]{0:T(1024)S(1)} %get-tuple-element.29, f32[768]{0:T(1024)S(1)} %get-tuple-element.20, ...), kind=kOutput, calls=%fused_computation.240 | convolution fusion | flops 476086272 | bytes 8104960 | tf_op jit(solution)/shard_map/dot_general | solution.py:89
  119.8 6.7 %constant_dynamic-update-slice_fusion.9 = (bf16[768,1024]{1,0:T(8,128)(2,1)S(1)}, bf16[768,128]{1,0:T(8,128)(2,1)}) fusion(bf16[768,1024]{1,0:T(8,128)(2,1)S(1)} %get-tuple-element.45, bf16[2304,256]{1,0:T(8,128)(2,1)} %constant_dynamic-update-slice_fusion.3, f32[768]{0:T(1024)S(1)} %get-tuple-element.30, f32[768]{0:T(1024)S(1)} %get-tuple-element.21, ...), kind=kOutput, calls=%fused_computation.239 | convolution fusion | flops 476086272 | bytes 8104960 | tf_op jit(solution)/shard_map/dot_general | solution.py:89
  126.5 6.7 %constant_dynamic-update-slice_fusion.8 = (bf16[768,1024]{1,0:T(8,128)(2,1)S(1)}, bf16[768,128]{1,0:T(8,128)(2,1)}) fusion(bf16[768,1024]{1,0:T(8,128)(2,1)S(1)} %get-tuple-element.47, bf16[2304,256]{1,0:T(8,128)(2,1)} %constant_dynamic-update-slice_fusion.3, f32[768]{0:T(1024)S(1)} %get-tuple-element.31, f32[768]{0:T(1024)S(1)} %get-tuple-element.22, ...), kind=kOutput, calls=%fused_computation.238 | convolution fusion | flops 476086272 | bytes 8104960 | tf_op jit(solution)/shard_map/dot_general | solution.py:89
  133.2 6.2 %constant_dynamic-update-slice_fusion.7 = (bf16[768,1024]{1,0:T(8,128)(2,1)S(1)}, bf16[768,128]{1,0:T(8,128)(2,1)S(1)}) fusion(bf16[768,1024]{1,0:T(8,128)(2,1)S(1)} %get-tuple-element.49, bf16[2304,256]{1,0:T(8,128)(2,1)} %constant_dynamic-update-slice_fusion.3, f32[768]{0:T(1024)S(1)} %get-tuple-element.26, f32[768]{0:T(1024)S(1)} %get-tuple-element.23, ...), kind=kOutput, calls=%fused_computation.237 | convolution fusion | flops 476086272 | bytes 8104960 | tf_op jit(solution)/shard_map/dot_general | solution.py:89
  139.5 11.1 %convolution_convert_fusion = bf16[768,1024]{1,0:T(8,128)(2,1)S(1)} fusion(bf16[768,4096]{1,0:T(8,128)(2,1)} %all-gather.2.cloned.1.call-done, bf16[1024,4096]{1,0:T(8,128)(2,1)} %param.9), kind=kOutput, calls=%fused_computation.102 | convolution fusion | flops 6443237376 | bytes 16252928 | tf_op jit(solution)/shard_map/dot_general | solution.py:27
  150.6 9.3 %multiply_reduce_fusion = (f32[768]{0:T(1024)}, f32[768]{0:T(1024)}, f32[768]{0:T(1024)}, f32[768]{0:T(1024)}, f32[768]{0:T(1024)}, /*index=5*/f32[768]{0:T(1024...) fusion(bf16[768,1024]{1,0:T(8,128)(2,1)S(1)} %convolution_convert_fusion, bf16[768,128]{1,0:T(8,128)(2,1)S(1)} %copy-done.42, ...), kind=kOutput, calls=%fused_computation.148 | convolution fusion | flops 479225856 | bytes 10871040 | tf_op jit(solution)/shard_map/dot_general | solution.py:89
  160.1 10.4 %convolution_bitcast_fusion = f32[4096,1024]{0,1:T(8,128)} fusion(bf16[768,1024]{1,0:T(8,128)(2,1)S(1)} %constant_dynamic-update-slice_fusion.6, bf16[768,4096]{1,0:T(8,128)(2,1)S(1)} %bitcast.209), kind=kOutput, calls=%fused_computation.2 | convolution fusion | flops 6442450944 | bytes 24641536 | tf_op jit(solution)/shard_map/dot_general | solution.py:21
  170.5 10.1 %fusion.38 = f32[2304,128]{0,1:T(8,128)S(1)} fusion(bf16[768,1024]{1,0:T(8,128)(2,1)} %copy-done.37, f32[2304,768]{1,0:T(8,128)} %fusion.116, f32[768]{0:T(1024)S(1)} %get-tuple-element.30, f32[768]{0:T(1024)S(1)} %get-tuple-element.21, s32[768]{0:T(1024)S(1)} %copy-done.12, s32[2304]{0:T(1024)S(1)} %iota_add_fusion, s32[768]{0:T(1024)S(1)} %iota_add_fusion.1, ...), kind=kOutput, calls=%fused_computation.85 | convolution fusion | flops 475987968 | bytes 8487168 | tf_op jit(solution)/shard_map/dot_general | solution.py:21
  217.1 7.0 %multiply_convert_fusion.7 = bf16[768,2304]{0,1:T(8,128)(2,1)S(1)} fusion(f32[768]{0:T(1024)S(1)} %copy-done.58, bf16[768,1024]{1,0:T(8,128)(2,1)S(1)} %copy-done.38, bf16[2304,256]{1,0:T(8,128)(2,1)} %constant_dynamic-update-slice_fusion.3, f32[768]{0:T(1024)S(1)} %copy-done.50, f32[768]{0:T(1024)S(1)} %copy-done.46, f32[2304,768]{1,0:T(8,128)S(1)} %bitcast.205, ...), kind=kOutput, calls=%fused_computation.25 | convolution fusion | flops 479526912 | bytes 11451392 | tf_op jit(solution)/shard_map/dot_general | solution.py:27
  225.5 6.7 %multiply_convert_fusion.6 = bf16[768,2304]{0,1:T(8,128)(2,1)S(1)} fusion(f32[768]{0:T(1024)S(1)} %copy-done.57, bf16[768,1024]{1,0:T(8,128)(2,1)S(1)} %copy-done.38, bf16[2304,256]{1,0:T(8,128)(2,1)} %constant_dynamic-update-slice_fusion.3, f32[768]{0:T(1024)S(1)} %copy-done.36, f32[768]{0:T(1024)S(1)} %copy-done.32, f32[2304,768]{1,0:T(8,128)S(1)} %bitcast.207, ...), kind=kOutput, calls=%fused_computation.23 | convolution fusion | flops 479526912 | bytes 11451392 | tf_op jit(solution)/shard_map/dot_general | solution.py:27
  233.6 6.6 %multiply_convert_fusion.5 = bf16[768,2304]{0,1:T(8,128)(2,1)S(1)} fusion(f32[768]{0:T(1024)S(1)} %copy-done.56, bf16[768,1024]{1,0:T(8,128)(2,1)S(1)} %copy-done.38, bf16[2304,256]{1,0:T(8,128)(2,1)} %constant_dynamic-update-slice_fusion.3, f32[768]{0:T(1024)S(1)} %copy-done.34, f32[768]{0:T(1024)S(1)} %copy-done.28, f32[2304,768]{1,0:T(8,128)S(1)} %bitcast.203, ...), kind=kOutput, calls=%fused_computation.21 | convolution fusion | flops 479526912 | bytes 11451392 | tf_op jit(solution)/shard_map/dot_general | solution.py:27
  241.6 6.8 %multiply_convert_fusion.4 = bf16[768,2304]{0,1:T(8,128)(2,1)S(1)} fusion(f32[768]{0:T(1024)S(1)} %copy-done.55, bf16[768,1024]{1,0:T(8,128)(2,1)S(1)} %copy-done.38, bf16[2304,256]{1,0:T(8,128)(2,1)} %constant_dynamic-update-slice_fusion.3, f32[768]{0:T(1024)S(1)} %copy-done.30, f32[768]{0:T(1024)S(1)} %copy-done.24, f32[2304,768]{1,0:T(8,128)S(1)} %bitcast.199, ...), kind=kOutput, calls=%fused_computation.19 | convolution fusion | flops 479526912 | bytes 11451392 | tf_op jit(solution)/shard_map/dot_general | solution.py:27
  249.9 6.8 %multiply_convert_fusion.3 = bf16[768,2304]{0,1:T(8,128)(2,1)S(1)} fusion(f32[768]{0:T(1024)S(1)} %copy-done.54, bf16[768,1024]{1,0:T(8,128)(2,1)S(1)} %copy-done.38, bf16[2304,256]{1,0:T(8,128)(2,1)} %constant_dynamic-update-slice_fusion.3, f32[768]{0:T(1024)S(1)} %copy-done.26, f32[768]{0:T(1024)S(1)} %copy-done.20, f32[2304,768]{1,0:T(8,128)S(1)} %bitcast.195, ...), kind=kOutput, calls=%fused_computation.17 | convolution fusion | flops 479526912 | bytes 11451392 | tf_op jit(solution)/shard_map/dot_general | solution.py:27
  258.1 7.1 %multiply_convert_fusion.2 = bf16[768,2304]{0,1:T(8,128)(2,1)S(1)} fusion(f32[768]{0:T(1024)S(1)} %copy-done.53, bf16[768,1024]{1,0:T(8,128)(2,1)} %copy-done.37, bf16[2304,256]{1,0:T(8,128)(2,1)} %constant_dynamic-update-slice_fusion.3, f32[768]{0:T(1024)S(1)} %copy-done.22, f32[768]{0:T(1024)S(1)} %copy-done.18, f32[2304,768]{1,0:T(8,128)S(1)} %bitcast.191, ...), kind=kOutput, calls=%fused_computation.15 | convolution fusion | flops 479526912 | bytes 11439360 | tf_op jit(solution)/shard_map/dot_general | solution.py:27
  274.6 6.9 %multiply_convert_fusion.1 = bf16[768,2304]{0,1:T(8,128)(2,1)S(1)} fusion(f32[768]{0:T(1024)S(1)} %copy-done.52, bf16[768,1024]{1,0:T(8,128)(2,1)} %copy-done.37, bf16[2304,256]{1,0:T(8,128)(2,1)} %constant_dynamic-update-slice_fusion.3, f32[768]{0:T(1024)S(1)} %copy-done.16, f32[768]{0:T(1024)S(1)} %copy-done.14, f32[2304,768]{1,0:T(8,128)S(1)} %bitcast.187, ...), kind=kOutput, calls=%fused_computation.13 | convolution fusion | flops 479526912 | bytes 11439360 | tf_op jit(solution)/shard_map/dot_general | solution.py:27
  282.9 6.8 %multiply_convert_fusion = bf16[768,2304]{0,1:T(8,128)(2,1)S(1)} fusion(f32[768]{0:T(1024)S(1)} %copy-done.51, bf16[768,1024]{1,0:T(8,128)(2,1)} %copy-done.37, bf16[2304,256]{1,0:T(8,128)(2,1)} %constant_dynamic-update-slice_fusion.3, f32[768]{0:T(1024)S(1)} %copy-done.48, f32[768]{0:T(1024)S(1)} %copy-done.44, f32[2304,768]{1,0:T(8,128)S(1)} %bitcast.213, ...), kind=kOutput, calls=%fused_computation.11 | convolution fusion | flops 479526912 | bytes 11439360 | tf_op jit(solution)/shard_map/dot_general | solution.py:27
  306.1 62.4 %collective-permute-done.7 = f32[768,256]{0,1:T(8,128)} collective-permute-done((f32[768,256]{0,1:T(8,128)}, f32[768,256]{0,1:T(8,128)}, u32[]{:S(2)}, u32[]{:S(2)}) %collective-permute-start.7) | collective-permute-done | bytes 786464 | tf_op jit(solution)/shard_map/ppermute | solution.py:17
  371.0 27.3 %reduce-scatter.2.cloned.1.call-done = f32[512,1024]{0,1:T(8,128)} async-done(((f32[4096,1024]{0,1:T(8,128)}), f32[512,1024]{0,1:T(8,128)}) %reduce-scatter.2.cloned.1.call-update) | async-done | bytes 2097168 | tf_op jit(solution)/shard_map/reduce_scatter | solution.py:100
  (265 shorter events, 115.6 us)
Async XLA Ops:
  7.2 132.3 %all-gather.2.cloned.1.call-start = ((), (), s32[]{:S(2)}) async-start(), calls=%async_computation.1 | async-start | bytes 7864320 | tf_op jit(solution)/shard_map/all_gather | solution.py:76
  7.2 16.0 %collective-permute-start = (s32[768]{0:T(1024)}, s32[768]{0:T(1024)S(1)}, u32[]{:S(2)}, u32[]{:S(2)}) collective-permute-start(s32[768]{0:T(1024)} %param.11), channel_id=1, source_target_pairs={{0,8},{4,12},{8,16},{12,20},{16,24},{20,28},{1,9},{5,13},{9,17},{1... | collective-permute-start | bytes 9224 | tf_op jit(solution)/shard_map/ppermute | solution.py:17
  12.1 12.8 %collective-permute-start.1 = (s32[768]{0:T(1024)}, s32[768]{0:T(1024)S(1)}, u32[]{:S(2)}, u32[]{:S(2)}) collective-permute-start(s32[768]{0:T(1024)} %param.11), channel_id=1, source_target_pairs={{0,4},{4,8},{8,12},{12,16},{16,20},{20,24},{24,28},{1,5},{5,9},{9,... | collective-permute-start | bytes 9224 | tf_op jit(solution)/shard_map/ppermute | solution.py:17
  13.6 13.1 %collective-permute-start.2 = (bf16[768,256]{1,0:T(8,128)(2,1)}, bf16[768,256]{1,0:T(8,128)(2,1)S(1)}, u32[]{:S(2)}, u32[]{:S(2)}) collective-permute-start(bf16[768,256]{1,0:T(8,128)(2,1)} %param.7), channel_id=1, source_target_pairs={{0,8},{4,12},{8,16},{12,20},{16,24},{20,28},{1,9},{5,13},{9,17},{1... | collective-permute-start | bytes 1179656 | tf_op jit(solution)/shard_map/ppermute | solution.py:17
  17.6 9.2 %collective-permute-start.3 = (bf16[768,256]{1,0:T(8,128)(2,1)}, bf16[768,256]{1,0:T(8,128)(2,1)S(1)}, u32[]{:S(2)}, u32[]{:S(2)}) collective-permute-start(bf16[768,256]{1,0:T(8,128)(2,1)} %param.7), channel_id=1, source_target_pairs={{0,4},{4,8},{8,12},{12,16},{16,20},{20,24},{24,28},{1,5},{5,9},{9,... | collective-permute-start | bytes 1179656 | tf_op jit(solution)/shard_map/ppermute | solution.py:17
  21.0 377.3 %reduce-scatter.2.cloned.1.call-start = ((), (), s32[]{:S(2)}) async-start(), calls=%async_computation.2 | async-start | bytes 18874368 | tf_op jit(solution)/shard_map/reduce_scatter | solution.py:100
  21.0 22.7 %collective-permute-start.4 = (bf16[768,256]{1,0:T(8,128)(2,1)}, bf16[768,256]{1,0:T(8,128)(2,1)S(1)}, u32[]{:S(2)}, u32[]{:S(2)}) collective-permute-start(bf16[768,256]{1,0:T(8,128)(2,1)} %param.8), channel_id=1, source_target_pairs={{0,8},{4,12},{8,16},{12,20},{16,24},{20,28},{1,9},{5,13},{9,17},{1... | collective-permute-start | bytes 1179656 | tf_op jit(solution)/shard_map/ppermute | solution.py:17
  23.3 22.3 %collective-permute-start.5 = (bf16[768,256]{1,0:T(8,128)(2,1)}, bf16[768,256]{1,0:T(8,128)(2,1)S(1)}, u32[]{:S(2)}, u32[]{:S(2)}) collective-permute-start(bf16[768,256]{1,0:T(8,128)(2,1)} %param.8), channel_id=1, source_target_pairs={{0,4},{4,8},{8,12},{12,16},{16,20},{20,24},{24,28},{1,5},{5,9},{9,... | collective-permute-start | bytes 1179656 | tf_op jit(solution)/shard_map/ppermute | solution.py:17
  38.2 88.3 %copy-start.1 = (f32[2304,768]{1,0:T(8,128)}, f32[2304,768]{1,0:T(8,128)S(1)}, u32[]{:S(2)}) copy-start(f32[2304,768]{1,0:T(8,128)S(1)} %fusion.112) | copy-start | bytes 21233668
  39.3 93.9 %copy-start = (f32[2304,768]{1,0:T(8,128)}, f32[2304,768]{1,0:T(8,128)S(1)}, u32[]{:S(2)}) copy-start(f32[2304,768]{1,0:T(8,128)S(1)} %fusion.109) | copy-start | bytes 21233668
  54.8 139.7 %copy-start.43 = (f32[768]{0:T(1024)}, f32[768]{0:T(1024)S(1)}, u32[]{:S(2)}) copy-start(f32[768]{0:T(1024)S(1)} %get-tuple-element.24) | copy-start | bytes 9220
  75.8 30.4 %copy-start.27 = (f32[768]{0:T(1024)}, f32[768]{0:T(1024)S(1)}, u32[]{:S(2)}) copy-start(f32[768]{0:T(1024)S(1)} %get-tuple-element.19) | copy-start | bytes 9220
  75.9 36.7 %copy-start.23 = (f32[768]{0:T(1024)}, f32[768]{0:T(1024)S(1)}, u32[]{:S(2)}) copy-start(f32[768]{0:T(1024)S(1)} %get-tuple-element.20) | copy-start | bytes 9220
  75.9 94.6 %copy-start.19 = (f32[768]{0:T(1024)}, f32[768]{0:T(1024)S(1)}, u32[]{:S(2)}) copy-start(f32[768]{0:T(1024)S(1)} %get-tuple-element.21) | copy-start | bytes 9220
  75.9 109.3 %copy-start.17 = (f32[768]{0:T(1024)}, f32[768]{0:T(1024)S(1)}, u32[]{:S(2)}) copy-start(f32[768]{0:T(1024)S(1)} %get-tuple-element.22) | copy-start | bytes 9220
  75.9 113.9 %copy-start.13 = (f32[768]{0:T(1024)}, f32[768]{0:T(1024)S(1)}, u32[]{:S(2)}) copy-start(f32[768]{0:T(1024)S(1)} %get-tuple-element.23) | copy-start | bytes 9220
  75.9 118.6 %copy-start.47 = (f32[768]{0:T(1024)}, f32[768]{0:T(1024)S(1)}, u32[]{:S(2)}) copy-start(f32[768]{0:T(1024)S(1)} %get-tuple-element.16) | copy-start | bytes 9220
  100.1 70.4 %copy-start.25 = (f32[768]{0:T(1024)}, f32[768]{0:T(1024)S(1)}, u32[]{:S(2)}) copy-start(f32[768]{0:T(1024)S(1)} %get-tuple-element.30) | copy-start | bytes 9220
  100.1 85.1 %copy-start.21 = (f32[768]{0:T(1024)}, f32[768]{0:T(1024)S(1)}, u32[]{:S(2)}) copy-start(f32[768]{0:T(1024)S(1)} %get-tuple-element.31) | copy-start | bytes 9220
  100.1 89.7 %copy-start.15 = (f32[768]{0:T(1024)}, f32[768]{0:T(1024)S(1)}, u32[]{:S(2)}) copy-start(f32[768]{0:T(1024)S(1)} %get-tuple-element.26) | copy-start | bytes 9220
  214.4 86.0 %collective-permute-start.8 = (f32[768,256]{0,1:T(8,128)}, f32[768,256]{0,1:T(8,128)}, u32[]{:S(2)}, u32[]{:S(2)}) collective-permute-start(f32[768,256]{0,1:T(8,128)} %get-tuple-element.32), channel_id=1, source_target_pairs={{4,0},{8,4},{12,8},{16,12},{20,16},{24,20},{28,24},{5,1},{9,5},{13... | collective-permute-start | bytes 2359304 | tf_op jit(solution)/shard_map/ppermute | solution.py:17
  215.7 84.7 %collective-permute-start.9 = (f32[768,256]{0,1:T(8,128)}, f32[768,256]{0,1:T(8,128)}, u32[]{:S(2)}, u32[]{:S(2)}) collective-permute-start(f32[768,256]{0,1:T(8,128)} %get-tuple-element.33), channel_id=1, source_target_pairs={{8,0},{12,4},{16,8},{20,12},{24,16},{28,20},{9,1},{13,5},{17,9},{2... | collective-permute-start | bytes 2359304 | tf_op jit(solution)/shard_map/ppermute | solution.py:17
  292.3 13.8 %collective-permute-start.6 = (f32[768,256]{0,1:T(8,128)}, f32[768,256]{0,1:T(8,128)}, u32[]{:S(2)}, u32[]{:S(2)}) collective-permute-start(f32[768,256]{0,1:T(8,128)} %get-tuple-element.34), channel_id=1, source_target_pairs={{4,0},{8,4},{12,8},{16,12},{20,16},{24,20},{28,24},{5,1},{9,5},{13... | collective-permute-start | bytes 2359304 | tf_op jit(solution)/shard_map/ppermute | solution.py:17
  293.7 74.8 %collective-permute-start.7 = (f32[768,256]{0,1:T(8,128)}, f32[768,256]{0,1:T(8,128)}, u32[]{:S(2)}, u32[]{:S(2)}) collective-permute-start(f32[768,256]{0,1:T(8,128)} %get-tuple-element.35), channel_id=1, source_target_pairs={{8,0},{12,4},{16,8},{20,12},{24,16},{28,20},{9,1},{13,5},{17,9},{2... | collective-permute-start | bytes 2359304 | tf_op jit(solution)/shard_map/ppermute | solution.py:17
  (77 other events, 671.8 us)
Sparse Core Ops, SparseCore 0:
  21.1 68.3 all-gather.1
  170.6 227.6 reduce-scatter.1
where the time goes:
time: 414 us; the launch traced here: 408 us
  matrix products  241 us (58%)
  waiting for transfers between devices  92.3 us (22%)
  other arithmetic  25.9 us (6%)
  starting transfers between devices  22.9 us (6%)
  between operations  15.8 us (4%)
  local copies, waits for them, and re-layouts  10 us (2%)
    dot_general x17, matrix products, contract_last(): lax.dot_general(left, right, (((1,), (1,)), ((), ())), preferred_element_...  111 us
    ppermute x10, waiting for transfers between devices, shifted(): lax.ppermute(value, axis, [(source, source + steps) for source in range(i...  64.9 us
    dot_general x17, matrix products, contract_rows(): lax.dot_general(left, right, (((0,), (0,)), ((), ())), preferred_element_...  62.9 us
    dot_general x8, matrix products, local(): jnp.dot(probs.astype(jnp.bfloat16), v_group, preferred_element_type=jnp.f...  56.5 us
    reduce_scatter x1, waiting for transfers between devices, local(): lax.psum_scatter(contract_rows(grad_full, attn_all), 'seq', scatter_dimen...  27.3 us
    ppermute x10, starting transfers between devices, shifted(): lax.ppermute(value, axis, [(source, source + steps) for source in range(i...  22.8 us
    reduce_sum x1, other arithmetic, head_probs(): return expo / jnp.sum(expo, axis=1, keepdims=True)  16 us
    dot_general x8, matrix products, head_grads(): jnp.dot(d_score, k_group, preferred_element_type=jnp.float32) * scale  11.1 us
  transfers between devices with their start and end apart: 12, of which 4 were waited for; matrix products, arithmetic and copies ran while one was open for 60% of the time, Pallas kernels for 0%

commit v1 on v0

v1 whole, which is shorter than its diff:
```python
import functools
import math

import jax
import jax.numpy as jnp
from jax import lax
from jax.experimental import pallas as pl
from jax.experimental.pallas import tpu as pltpu
from jax.sharding import PartitionSpec as P

HEAD_SIZE = 128
TILE = 256
NEG_BIG = -1e30
VMEM_BYTES = 50 * 1024 * 1024


def mm(left, right, left_dim, right_dim):
    return lax.dot_general(
        left, right, (((left_dim,), (right_dim,)), ((), ())), preferred_element_type=jnp.float32
    )


def params(count):
    return pltpu.CompilerParams(
        dimension_semantics=("arbitrary",) * count, vmem_limit_bytes=VMEM_BYTES
    )


def lane_heads(ref, factor):
    return jnp.concatenate(
        [ref[:, h * HEAD_SIZE : (h + 1) * HEAD_SIZE] for h in range(factor)], axis=0
    )


def assemble(target, parts, tok):
    for index, part in enumerate(parts):
        target[index * tok : (index + 1) * tok, :] = part[...]


def visible_tile(limit, j, last):
    rows = lax.broadcasted_iota(jnp.int32, (TILE, TILE), 0)
    seen = rows >= limit - j * TILE
    if j == last:
        seen = seen & (rows <= lax.broadcasted_iota(jnp.int32, (TILE, TILE), 1))
    return seen


def forward_kernel(
    tok, factor, low_ref, q_ref, kd, kn, ko, vd, vn, vo, attn_ref, lse_ref, k_scr, v_scr, vt_scr
):
    step = pl.program_id(1)
    scale = math.log2(math.e) / math.sqrt(HEAD_SIZE)

    @pl.when(step == 0)
    def _():
        assemble(k_scr, (kd, kn, ko), tok)
        assemble(v_scr, (vd, vn, vo), tok)
        vt_scr[...] = v_scr[...].T

    tiles = 2 * tok // TILE + 1
    base = pl.multiple_of(step * TILE, TILE)
    limit = low_ref[...] - base
    for h in range(factor):
        q_head = q_ref[:, h * HEAD_SIZE : (h + 1) * HEAD_SIZE]
        scores = []
        top = None
        for j in range(tiles):
            k_tile = k_scr[pl.ds(pl.multiple_of(base + j * TILE, TILE), TILE), :]
            raw = mm(k_tile, q_head, 1, 1)
            raw = jnp.where(visible_tile(limit, j, tiles - 1), raw, NEG_BIG)
            scores.append(raw)
            high = jnp.max(raw, axis=0, keepdims=True)
            top = high if top is None else jnp.maximum(top, high)
        shift = top * scale
        total = None
        low_parts = []
        for j in range(tiles):
            expo = jnp.exp2(scores[j] * scale - shift)
            part = jnp.sum(expo, axis=0, keepdims=True)
            total = part if total is None else total + part
            low_parts.append(expo.astype(jnp.bfloat16))
        weights = jnp.concatenate(low_parts, axis=0)
        vt = vt_scr[:, pl.ds(base, tiles * TILE)]
        out_t = mm(vt, weights, 1, 0) / total
        attn_ref[:, h * HEAD_SIZE : (h + 1) * HEAD_SIZE] = out_t.T.astype(jnp.bfloat16)
        lse_ref[0, h : h + 1, :] = shift + jnp.log2(total)


def backward_kernel(
    tok, factor, low_ref, lse_ref, q_ref, do_ref, at_ref, kd, kn, ko, vd, vn, vo,
    dq_ref, own_ref, far_ref, k_scr, v_scr, kt_scr, dk_scr, dv_scr, dq_scr,
):
    step = pl.program_id(0)
    scale = math.log2(math.e) / math.sqrt(HEAD_SIZE)
    plain = 1.0 / math.sqrt(HEAD_SIZE)

    @pl.when(step == 0)
    def _():
        assemble(k_scr, (kd, kn, ko), tok)
        assemble(v_scr, (vd, vn, vo), tok)
        kt_scr[...] = k_scr[...].T
        dk_scr[...] = jnp.zeros_like(dk_scr)
        dv_scr[...] = jnp.zeros_like(dv_scr)

    tiles = 2 * tok // TILE + 1
    base = pl.multiple_of(step * TILE, TILE)
    limit = low_ref[...] - base
    q_stack = lane_heads(q_ref, factor)
    do_stack = lane_heads(do_ref, factor)
    at_stack = lane_heads(at_ref, factor)
    product = do_stack.astype(jnp.float32) * at_stack.astype(jnp.float32)
    delta = jnp.sum(product.T, axis=0, keepdims=True)
    for j in range(tiles):
        rows = pl.ds(pl.multiple_of(base + j * TILE, TILE), TILE)
        k_tile = k_scr[rows, :]
        v_tile = v_scr[rows, :]
        seen = visible_tile(limit, j, tiles - 1)
        probs_parts = []
        score_parts = []
        for h in range(factor):
            part = slice(h * TILE, (h + 1) * TILE)
            raw = mm(k_tile, q_stack[part], 1, 1)
            d_prob = mm(v_tile, do_stack[part], 1, 1)
            probs = jnp.exp2(raw * scale - lse_ref[0, h : h + 1, :])
            probs = jnp.where(seen, probs, 0.0)
            probs_parts.append(probs.astype(jnp.bfloat16))
            score_parts.append((probs * (d_prob - delta[:, part])).astype(jnp.bfloat16))
        probs_all = jnp.concatenate(probs_parts, axis=1)
        score_all = jnp.concatenate(score_parts, axis=1)
        dv_scr[rows, :] += mm(probs_all, do_stack, 1, 0)
        dk_scr[rows, :] += mm(score_all, q_stack, 1, 0)
        kt = kt_scr[:, pl.ds(pl.multiple_of(base + j * TILE, TILE), TILE)]
        gain = mm(kt, score_all, 1, 0)
        if j == 0:
            dq_scr[...] = gain
        else:
            dq_scr[...] += gain
    for h in range(factor):
        piece = dq_scr[:, h * TILE : (h + 1) * TILE] * plain
        dq_ref[:, h * HEAD_SIZE : (h + 1) * HEAD_SIZE] = piece.T.astype(jnp.bfloat16)

    @pl.when(step == pl.num_programs(0) - 1)
    def _():
        own_ref[:, :HEAD_SIZE] = dk_scr[2 * tok :, :] * plain
        own_ref[:, HEAD_SIZE:] = dv_scr[2 * tok :, :]
        far_ref[:, :HEAD_SIZE] = (dk_scr[: 2 * tok, :] * plain).astype(jnp.bfloat16)
        far_ref[:, HEAD_SIZE:] = dv_scr[: 2 * tok, :].astype(jnp.bfloat16)


def key_specs(tok, kv_heads, column):
    specs = []
    for offset in (0, kv_heads):
        for _ in range(3):
            specs.append(
                pl.BlockSpec((tok, HEAD_SIZE), functools.partial(column, offset))
            )
    return specs


def forward(low, queries, kv, tok, kv_heads, factor):
    tiles = 2 * tok // TILE + 1
    flops = 4 * tok * tiles * TILE * HEAD_SIZE * kv_heads * factor
    return pl.pallas_call(
        functools.partial(forward_kernel, tok, factor),
        grid=(kv_heads, tok // TILE),
        in_specs=[
            pl.BlockSpec((1, TILE), lambda g, i: (0, i)),
            pl.BlockSpec((TILE, factor * HEAD_SIZE), lambda g, i: (i, g)),
        ]
        + key_specs(tok, kv_heads, lambda offset, g, i: (0, g + offset)),
        out_specs=[
            pl.BlockSpec((TILE, factor * HEAD_SIZE), lambda g, i: (i, g)),
            pl.BlockSpec((1, factor, TILE), lambda g, i: (g, 0, i)),
        ],
        out_shape=[
            jax.ShapeDtypeStruct(queries.shape, jnp.bfloat16),
            jax.ShapeDtypeStruct((kv_heads, factor, tok), jnp.float32),
        ],
        scratch_shapes=[
            pltpu.VMEM((3 * tok, HEAD_SIZE), jnp.bfloat16),
            pltpu.VMEM((3 * tok, HEAD_SIZE), jnp.bfloat16),
            pltpu.VMEM((HEAD_SIZE, 3 * tok), jnp.bfloat16),
        ],
        compiler_params=params(2),
        cost_estimate=pl.CostEstimate(
            flops=4 * flops, bytes_accessed=8 * 2**20, transcendentals=0
        ),
        name="attention_forward",
    )(low, queries, *(kv * 2))


def backward(group, low, lse, queries, d_attn, attn, kv, tok, kv_heads, factor):
    tiles = 2 * tok // TILE + 1
    flops = 10 * tok * tiles * TILE * HEAD_SIZE * factor
    wide = pl.BlockSpec((TILE, factor * HEAD_SIZE), lambda i: (i, group))
    whole = lambda i: (0, 0)
    return pl.pallas_call(
        functools.partial(backward_kernel, tok, factor),
        grid=(tok // TILE,),
        in_specs=[
            pl.BlockSpec((1, TILE), lambda i: (0, i)),
            pl.BlockSpec((1, factor, TILE), lambda i: (group, 0, i)),
            wide,
            wide,
            wide,
        ]
        + key_specs(tok, kv_heads, lambda offset, i: (0, group + offset)),
        out_specs=[
            pl.BlockSpec((TILE, factor * HEAD_SIZE), lambda i: (i, 0)),
            pl.BlockSpec((tok, 2 * HEAD_SIZE), whole),
            pl.BlockSpec((2 * tok, 2 * HEAD_SIZE), whole),
        ],
        out_shape=[
            jax.ShapeDtypeStruct((tok, factor * HEAD_SIZE), jnp.bfloat16),
            jax.ShapeDtypeStruct((tok, 2 * HEAD_SIZE), jnp.float32),
            jax.ShapeDtypeStruct((2 * tok, 2 * HEAD_SIZE), jnp.bfloat16),
        ],
        scratch_shapes=[
            pltpu.VMEM((3 * tok, HEAD_SIZE), jnp.bfloat16),
            pltpu.VMEM((3 * tok, HEAD_SIZE), jnp.bfloat16),
            pltpu.VMEM((HEAD_SIZE, 3 * tok), jnp.bfloat16),
            pltpu.VMEM((3 * tok, HEAD_SIZE), jnp.float32),
            pltpu.VMEM((3 * tok, HEAD_SIZE), jnp.float32),
            pltpu.VMEM((HEAD_SIZE, factor * TILE), jnp.float32),
        ],
        compiler_params=params(1),
        cost_estimate=pl.CostEstimate(
            flops=3 * flops, bytes_accessed=8 * 2**20, transcendentals=0
        ),
        name="attention_backward",
    )(low, lse, queries, d_attn, attn, *(kv * 2))


def project_kernel(g_ref, w_ref, out_ref, acc):
    step = pl.program_id(0)
    gain = mm(g_ref[0], w_ref[...], 1, 1)

    @pl.when(step == 0)
    def _():
        acc[...] = gain

    @pl.when(step > 0)
    def _():
        acc[...] += gain

    @pl.when(step == pl.num_programs(0) - 1)
    def _():
        out_ref[...] = acc[...].astype(jnp.bfloat16)


def project(grads, out_weight):
    count, tok, width = grads.shape
    heads = out_weight.shape[0]
    return pl.pallas_call(
        project_kernel,
        grid=(count,),
        in_specs=[
            pl.BlockSpec((1, tok, width), lambda t: (t, 0, 0)),
            pl.BlockSpec((heads, width), lambda t: (0, t)),
        ],
        out_specs=pl.BlockSpec((tok, heads), lambda t: (0, 0)),
        out_shape=jax.ShapeDtypeStruct((tok, heads), jnp.bfloat16),
        scratch_shapes=[pltpu.VMEM((tok, heads), jnp.float32)],
        compiler_params=params(1),
        cost_estimate=pl.CostEstimate(
            flops=2 * tok * heads * width * count, bytes_accessed=16 * 2**20, transcendentals=0
        ),
        name="project_grad",
    )(grads, out_weight)


def weight_kernel(core_ref, at_ref, g_ref, out_ref, at_scr):
    @pl.when(pl.program_id(0) == 0)
    def _():
        at_scr[...] = at_ref[...].T

    out_ref[0] = mm(at_scr[...], g_ref[0], 1, 0).astype(jnp.bfloat16)


def weight_blocks(core, attn, grads, pairs):
    count, tok, width = grads.shape
    heads = attn.shape[1]
    columns = count * width // (2 * pairs)
    per = width // columns

    def pick(d, core_ref):
        block = 2 * d + core_ref[0]
        return (block // per, 0, block % per)

    return pl.pallas_call(
        weight_kernel,
        grid_spec=pltpu.PrefetchScalarGridSpec(
            num_scalar_prefetch=1,
            grid=(pairs,),
            in_specs=[
                pl.BlockSpec((tok, heads), lambda d, core_ref: (0, 0)),
                pl.BlockSpec((1, tok, columns), pick),
            ],
            out_specs=pl.BlockSpec((1, heads, columns), lambda d, core_ref: (d, 0, 0)),
            scratch_shapes=[pltpu.VMEM((heads, tok), jnp.bfloat16)],
        ),
        out_shape=jax.ShapeDtypeStruct((pairs, heads, columns), jnp.bfloat16),
        compiler_params=params(1),
        cost_estimate=pl.CostEstimate(
            flops=2 * tok * heads * columns * pairs, bytes_accessed=12 * 2**20, transcendentals=0
        ),
        name="weight_blocks",
    )(jnp.reshape(core, (1,)), attn, grads)


def local(queries, keys, values, out_weight, out_grad, doc_ids):
    tok = queries.shape[0]
    q_heads = queries.shape[1] // HEAD_SIZE
    kv_heads = keys.shape[1] // HEAD_SIZE
    factor = q_heads // kv_heads
    count = lax.axis_size("seq")
    pairs = count // 2
    shard = lax.axis_index("seq")
    core = shard % 2
    chip = shard // 2
    swap = [(s, s ^ 1) for s in range(count)]

    own = jnp.concatenate([keys, values], axis=1)
    ahead = [(s, s + 2) for s in range(count - 2)]
    to_odd = [(s, s + 1) for s in range(0, count, 2)]
    to_even = [(s + 1, s) for s in range(0, count, 2)]
    distant = lax.ppermute(own, "seq", ahead)
    from_even = lax.ppermute(own, "seq", to_odd)
    from_odd = lax.ppermute(distant, "seq", to_even)
    nearby = jnp.where(core == 1, from_even, from_odd)
    doc_far = lax.ppermute(doc_ids, "seq", ahead)
    doc_near = lax.ppermute(doc_ids, "seq", [(s, s + 1) for s in range(count - 1)])
    kv = (distant, nearby, own)
    grads = lax.all_gather(out_grad, "tensor", axis=0)

    doc_keys = jnp.concatenate([doc_far, doc_near, doc_ids])
    before = jnp.sum((doc_keys[:, None] < doc_ids[None, :]).astype(jnp.int32), axis=0)
    low = jnp.maximum(before, (2 - shard) * tok)
    low = jnp.maximum(low, jnp.arange(1, tok + 1, dtype=jnp.int32))[None, :]

    attn, lse = forward(low, queries, kv, tok, kv_heads, factor)
    sent = weight_blocks(1 - core, attn, grads, pairs)
    received = lax.ppermute(sent, "seq", swap)
    kept = weight_blocks(core, attn, grads, pairs)
    d_attn = project(grads, out_weight)

    def paired(index):
        index = jnp.clip(index, 0, pairs - 1)
        return lax.dynamic_index_in_dim(kept, index, 0, keepdims=False).astype(
            jnp.float32
        ) + lax.dynamic_index_in_dim(received, index, 0, keepdims=False).astype(jnp.float32)

    from_left = from_right = None
    for t in range(pairs - 1):
        right = paired(pairs - 1 - t + chip)
        left = paired(t - pairs + 1 + chip)
        if t:
            right = right + from_left.astype(jnp.float32)
            left = left + from_right.astype(jnp.float32)
        hops = [(2 * z + c, 2 * z + 2 + c) for z in range(t + 1) for c in range(2)]
        back = [(count - 1 - a, count - 1 - b) for a, b in hops]
        from_left = lax.ppermute(right.astype(jnp.bfloat16), "seq", hops)
        from_right = lax.ppermute(left.astype(jnp.bfloat16), "seq", back)
    weight_grad = paired(chip) + from_left.astype(jnp.float32) + from_right.astype(jnp.float32)

    dq_list = []
    totals = []
    for group in range(kv_heads):
        dq, own_part, far = backward(
            group, low, lse, queries, d_attn, attn, kv, tok, kv_heads, factor
        )
        dq_list.append(dq)
        swapped = lax.ppermute(far[tok:], "seq", swap).astype(jnp.float32)
        joined = far[:tok].astype(jnp.float32) + jnp.where(core == 1, swapped, 0.0)
        returned = lax.ppermute(
            joined.astype(jnp.bfloat16), "seq", [(s + 2, s) for s in range(count - 2)]
        )
        totals.append(
            own_part + jnp.where(core == 0, swapped, 0.0) + returned.astype(jnp.float32)
        )
    grad_queries = jnp.concatenate(dq_list, axis=1)
    grad_keys = jnp.concatenate([t[:, :HEAD_SIZE] for t in totals], axis=1)
    grad_values = jnp.concatenate([t[:, HEAD_SIZE:] for t in totals], axis=1)
    return (
        grad_queries,
        grad_keys.astype(jnp.bfloat16),
        grad_values.astype(jnp.bfloat16),
        weight_grad.astype(jnp.bfloat16),
    )


def solution(mesh):
    placed = (
        P("seq", "tensor"),
        P("seq", "tensor"),
        P("seq", "tensor"),
        P("tensor", None),
        P("seq", "tensor"),
        P("seq"),
    )
    return jax.shard_map(
        local,
        mesh=mesh,
        in_specs=placed,
        out_specs=(P("seq", "tensor"), P("seq", "tensor"), P("seq", "tensor"), P("tensor", "seq")),
        check_vma=False,
    )
```

time: 414 us -> 234 us (0.57); the launches traced: 408 us -> 233 us
  matrix products: 241 us -> 0 us
  Pallas kernels: 0 us -> 83.4 us
  starting transfers between devices: 22.9 us -> 35.4 us
  waiting for transfers between devices: 92.3 us -> 80.3 us
  other arithmetic: 25.9 us -> 17 us
  local copies, waits for them, and re-layouts: 10 us -> 2.1 us
    dot_general x50 -> x0, matrix products: 241 us -> none  [the longest x17 111 us: contract_last(): lax.dot_general(left, right, (((1,), (1,)), ((), ())), preferred_element_...]
    pallas_call x0 -> x6, Pallas kernels: none -> 83.4 us  [the longest x2 33.5 us: backward(): pl.pallas_call(functools.partial(backward_kernel, tok, factor), grid=(tok...]
    reduce_scatter x1 -> x0, waiting for transfers between devices: 27.3 us -> none  [local(): lax.psum_scatter(contract_rows(grad_full, attn_all), 'seq', scatter_dimen...]
    all_gather x1, waiting for transfers between devices: 0.02 us -> 15 us  [local(): grads = lax.all_gather(out_grad, 'tensor', axis=0)]
    reduce_sum x1, other arithmetic: 16 us -> 1.09 us  [local(): jnp.sum((doc_keys[:, None] < doc_ids[None, :]).astype(jnp.int32), axis=0)]
    ppermute x10 -> x16, starting transfers between devices: 22.8 us -> 35.3 us  [the longest x3 13.6 us: local(): from_left = lax.ppermute(right.astype(jnp.bfloat16), 'seq', hops)]
    convert_element_type x3 -> x7, other arithmetic: 6.55 us -> 13.2 us  [the longest x3 8.19 us: local(): from_left = lax.ppermute(right.astype(jnp.bfloat16), 'seq', hops)]
    unnamed x185 -> x19, local copies, waits for them, and re-layouts: 7.47 us -> 1.96 us
  transfers between devices with their start and end apart: 12 -> 17, of which waited for: 4 -> 10; matrix products, arithmetic and copies ran while one was open for 60% -> 5% of each run, Pallas kernels for 0% -> 33%
where the time goes in v1:
time: 234 us; the launch traced here: 233 us
  Pallas kernels  83.4 us (36%)
  waiting for transfers between devices  80.3 us (34%)
  starting transfers between devices  35.4 us (15%)
  other arithmetic  17 us (7%)
  between operations  14.5 us (6%)
    pallas_call x2, Pallas kernels, backward(): pl.pallas_call(functools.partial(backward_kernel, tok, factor), grid=(tok...  33.5 us
    pallas_call x1, Pallas kernels, forward(): pl.pallas_call(functools.partial(forward_kernel, tok, factor), grid=(kv_h...  24.8 us
    ppermute x3, waiting for transfers between devices, local(): from_left = lax.ppermute(right.astype(jnp.bfloat16), 'seq', hops)  23.4 us
    ppermute x1, waiting for transfers between devices, local(): distant = lax.ppermute(own, 'seq', ahead)  15.2 us
    all_gather x1, waiting for transfers between devices, local(): grads = lax.all_gather(out_grad, 'tensor', axis=0)  15 us
    pallas_call x2, Pallas kernels, weight_blocks(): pl.pallas_call(weight_kernel, grid_spec=pltpu.PrefetchScalarGridSpec(num_...  14.3 us
    ppermute x3, waiting for transfers between devices, local(): from_right = lax.ppermute(left.astype(jnp.bfloat16), 'seq', back)  13.6 us
    ppermute x3, starting transfers between devices, local(): from_left = lax.ppermute(right.astype(jnp.bfloat16), 'seq', hops)  13.6 us
  transfers between devices with their start and end apart: 17, of which 10 were waited for; matrix products, arithmetic and copies ran while one was open for 5% of the time, Pallas kernels for 33%

profile of v1, /device:TPU:0, one launch (start us, length us, event | category | flops | bytes accessed | tf_op | source)
XLA Modules:
  0.0 232.7 jit_solution(9119700031158241855)
XLA Ops:
  9.0 5.0 %collective-permute-start.2 = (bf16[768,512]{1,0:T(8,128)(2,1)S(1)}, bf16[768,512]{1,0:T(8,128)(2,1)S(1)}, u32[]{:S(2)}, u32[]{:S(2)}) collective-permute-start(bf16[768,512]{1,0:T(8,128)(2,1)S(1)} %constant_dynamic-update-slice_fusion.ko.vo), channel_id=1, source_target_pairs={{0,8},{4,12},{8,16},{12,20},{16,24},{20,28},{1,9},{5,13},{9,17},{1... | collective-permute-start | bytes 2359304 | tf_op jit(solution)/shard_map/ppermute | solution.py:327
  15.5 15.2 %collective-permute-done.2.kd.vd = bf16[768,512]{1,0:T(8,128)(2,1)S(1)} collective-permute-done((bf16[768,512]{1,0:T(8,128)(2,1)S(1)}, bf16[768,512]{1,0:T(8,128)(2,1)S(1)}, u32[]{:S(2)}, u32[]{:S(2)}) %collective-permute-start.2) | collective-permute-done | bytes 786464 | tf_op jit(solution)/shard_map/ppermute | solution.py:327
  32.9 3.1 %collective-permute-start.1 = (s32[768]{0:T(1024)S(1)}, s32[768]{0:T(1024)S(1)}, u32[]{:S(2)}, u32[]{:S(2)}) collective-permute-start(s32[768]{0:T(1024)S(1)} %copy-done.8), channel_id=1, source_target_pairs={{0,4},{4,8},{8,12},{12,16},{16,20},{20,24},{24,28},{1,5},{5,9},{9,... | collective-permute-start | bytes 9224 | tf_op jit(solution)/shard_map/ppermute | solution.py:332
  36.0 4.4 %collective-permute-start = (s32[768]{0:T(1024)S(1)}, s32[768]{0:T(1024)S(1)}, u32[]{:S(2)}, u32[]{:S(2)}) collective-permute-start(s32[768]{0:T(1024)S(1)} %copy-done.8), channel_id=1, source_target_pairs={{0,8},{4,12},{8,16},{12,20},{16,24},{20,28},{1,9},{5,13},{9,17},{1... | collective-permute-start | bytes 9224 | tf_op jit(solution)/shard_map/ppermute | solution.py:331
  43.0 24.8 %attention_forward.1 = (bf16[768,1024]{1,0:T(8,128)(2,1)S(1)}, f32[2,4,768]{2,1,0:T(4,128)S(1)}) custom-call(s32[1,768]{1,0:T(1,128)S(1)} %add_maximum_fusion.low_ref, bf16[768,1024]{1,0:T(8,128)(2,1)} %q_ref.5, bf16[768,512]{1,0:T(8,128)(2,1)S(1)} %copy-done.3, bf16[768,512]{1,0:T(8,128)(2,1)S(1)} %broadcast_select_fusion.kn.vn, ...), custom_call_target="tpu_custom_call" | custom-call | flops 22548578304 | bytes 8388608 | tf_op jit(solution)/shard_map/attention_forward/pallas_call | solution.py:163
  67.8 15.0 %all-gather.3.cloned.1.call-done = bf16[3072,1024]{1,0:T(8,128)(2,1)} async-done(((bf16[768,1024]{1,0:T(8,128)(2,1)}), bf16[3072,1024]{1,0:T(8,128)(2,1)}) %all-gather.3.cloned.1.call-update) | async-done | bytes 6291472 | tf_op jit(solution)/shard_map/all_gather | solution.py:334
  82.8 7.1 %weight_blocks.3 = bf16[4,1024,512]{2,1,0:T(8,128)(2,1)} custom-call(s32[1]{0:T(128)} %bitcast.2.core_ref, bf16[768,1024]{1,0:T(8,128)(2,1)S(1)} %get-tuple-element.13.at_ref, bf16[4,768,1024]{2,1,0:T(8,128)(2,1)} %bitcast.29), custom_call_target="tpu_custom_call" | custom-call | flops 3221225472 | bytes 12582912 | tf_op jit(solution)/shard_map/weight_blocks/pallas_call | solution.py:290
  89.9 7.2 %weight_blocks.2 = bf16[4,1024,512]{2,1,0:T(8,128)(2,1)} custom-call(s32[1]{0:T(128)} %bitcast.1.core_ref, bf16[768,1024]{1,0:T(8,128)(2,1)S(1)} %get-tuple-element.13.at_ref, bf16[4,768,1024]{2,1,0:T(8,128)(2,1)} %bitcast.30), custom_call_target="tpu_custom_call" | custom-call | flops 3221225472 | bytes 12582912 | tf_op jit(solution)/shard_map/weight_blocks/pallas_call | solution.py:290
  97.4 4.1 %fusion.6 = (bf16[1024,512]{1,0:T(8,128)(2,1)}, bf16[1024,512]{1,0:T(8,128)(2,1)}) fusion(bf16[4,1024,512]{2,1,0:T(8,128)(2,1)} %collective-permute-done.9, s32[]{:T(128)S(6)} %min.25, bf16[4,1024,512]{2,1,0:T(8,128)(2,1)} %weight_blocks.2, s32[]{:T(128)S(6)} %min.28), kind=kLoop, calls=%fused_computation.15 | loop fusion | flops 4194304 | bytes 6291464 | tf_op jit(solution)/shard_map/convert_element_type | solution.py:362
  101.5 3.4 %collective-permute-start.10 = (bf16[1024,512]{1,0:T(8,128)(2,1)}, bf16[1024,512]{1,0:T(8,128)(2,1)S(1)}, u32[]{:S(2)}, u32[]{:S(2)}) collective-permute-start(bf16[1024,512]{1,0:T(8,128)(2,1)} %get-tuple-element.22), channel_id=1, source_target_pairs={{0,8},{4,12},{1,9},{5,13},{2,10},{6,14},{3,11},{7,15}} | collective-permute-start | bytes 3145736 | tf_op jit(solution)/shard_map/ppermute | solution.py:362
  105.0 10.8 %project_grad.1.do_ref = bf16[768,1024]{1,0:T(8,128)(2,1)S(1)} custom-call(bf16[4,768,1024]{2,1,0:T(8,128)(2,1)} %bitcast.31, bf16[1024,4096]{1,0:T(8,128)(2,1)} %w_ref.1), custom_call_target="tpu_custom_call" | custom-call | flops 6442450944 | bytes 16777216 | tf_op jit(solution)/shard_map/project_grad/pallas_call | solution.py:254
  116.7 11.2 %collective-permute-done.10 = bf16[1024,512]{1,0:T(8,128)(2,1)S(1)} collective-permute-done((bf16[1024,512]{1,0:T(8,128)(2,1)}, bf16[1024,512]{1,0:T(8,128)(2,1)S(1)}, u32[]{:S(2)}, u32[]{:S(2)}) %collective-permute-start.10) | collective-permute-done | bytes 1048608 | tf_op jit(solution)/shard_map/ppermute | solution.py:362
  129.6 4.5 %collective-permute-start.11 = (bf16[1024,512]{1,0:T(8,128)(2,1)S(1)}, bf16[1024,512]{1,0:T(8,128)(2,1)S(1)}, u32[]{:S(2)}, u32[]{:S(2)}) collective-permute-start(bf16[1024,512]{1,0:T(8,128)(2,1)S(1)} %fusion.2), channel_id=1, source_target_pairs={{0,8},{4,12},{8,16},{12,20},{1,9},{5,13},{9,17},{13,21},{2,10},{6,... | collective-permute-start | bytes 3145736 | tf_op jit(solution)/shard_map/ppermute | solution.py:362
  134.1 16.8 %attention_backward.2 = (bf16[768,512]{1,0:T(8,128)(2,1)S(1)}, f32[768,256]{1,0:T(8,128)S(1)}, bf16[1536,256]{1,0:T(8,128)(2,1)S(1)}) custom-call(s32[1,768]{1,0:T(1,128)S(1)} %add_maximum_fusion.low_ref, f32[2,4,768]{2,1,0:T(4,128)S(1)} %get-tuple-element.12.lse_ref, bf16[768,1024]{1,0:T(8,128)(2,1)} %q_ref.5, bf16[768,1024]{1,0:T(8,128)(2,1)} %copy-done.5, ...), custom_call_target="tpu_custom_call" | custom-call | flops 21139292160 | bytes 8388608 | tf_op jit(solution)/shard_map/attention_backward/pallas_call | solution.py:197
  151.0 4.7 %collective-permute-done.11 = bf16[1024,512]{1,0:T(8,128)(2,1)S(1)} collective-permute-done((bf16[1024,512]{1,0:T(8,128)(2,1)S(1)}, bf16[1024,512]{1,0:T(8,128)(2,1)S(1)}, u32[]{:S(2)}, u32[]{:S(2)}) %collective-permute-start.11) | collective-permute-done | bytes 1048608 | tf_op jit(solution)/shard_map/ppermute | solution.py:362
  155.7 2.4 %fusion.3 = (bf16[1024,512]{1,0:T(8,128)(2,1)S(1)}, bf16[1024,512]{1,0:T(8,128)(2,1)S(1)}) fusion(bf16[1024,512]{1,0:T(8,128)(2,1)S(1)} %collective-permute-done.11, bf16[4,1024,512]{2,1,0:T(8,128)(2,1)} %collective-permute-done.9, s32[]{:T(128)S(6)} %min.23, bf16[4,1024,512]{2,1,0:T(8,128)(2,1)S(1)} %copy-done.6, ...), kind=kLoop, calls=%fused_computation.8 | loop fusion | flops 6291456 | bytes 8388616 | tf_op jit(solution)/shard_map/convert_element_type | solution.py:362
  159.8 16.7 %attention_backward.3 = (bf16[768,512]{1,0:T(8,128)(2,1)S(1)}, f32[768,256]{1,0:T(8,128)S(1)}, bf16[1536,256]{1,0:T(8,128)(2,1)S(1)}) custom-call(s32[1,768]{1,0:T(1,128)S(1)} %add_maximum_fusion.low_ref, f32[2,4,768]{2,1,0:T(4,128)S(1)} %get-tuple-element.12.lse_ref, bf16[768,1024]{1,0:T(8,128)(2,1)} %q_ref.5, bf16[768,1024]{1,0:T(8,128)(2,1)} %copy-done.5, ...), custom_call_target="tpu_custom_call" | custom-call | flops 21139292160 | bytes 8388608 | tf_op jit(solution)/shard_map/attention_backward/pallas_call | solution.py:197
  180.9 5.6 %collective-permute-start.12 = (bf16[1024,512]{1,0:T(8,128)(2,1)S(1)}, bf16[1024,512]{1,0:T(8,128)(2,1)S(1)}, u32[]{:S(2)}, u32[]{:S(2)}) collective-permute-start(bf16[1024,512]{1,0:T(8,128)(2,1)S(1)} %get-tuple-element.20), channel_id=1, source_target_pairs={{0,8},{4,12},{8,16},{12,20},{16,24},{20,28},{1,9},{5,13},{9,17},{1... | collective-permute-start | bytes 3145736 | tf_op jit(solution)/shard_map/ppermute | solution.py:362
  186.5 2.0 fusion.1
  189.8 2.6 %collective-permute-done.6 = bf16[768,256]{1,0:T(8,128)(2,1)S(1)} collective-permute-done((bf16[768,256]{1,0:T(8,128)(2,1)S(1)}, bf16[768,256]{1,0:T(8,128)(2,1)S(1)}, u32[]{:S(2)}, u32[]{:S(2)}) %collective-permute-start.6) | collective-permute-done | bytes 393248 | tf_op jit(solution)/shard_map/ppermute | solution.py:375
  192.6 8.2 %collective-permute-done.8 = bf16[768,256]{1,0:T(8,128)(2,1)S(1)} collective-permute-done((bf16[768,256]{1,0:T(8,128)(2,1)S(1)}, bf16[768,256]{1,0:T(8,128)(2,1)S(1)}, u32[]{:S(2)}, u32[]{:S(2)}) %collective-permute-start.8) | collective-permute-done | bytes 393248 | tf_op jit(solution)/shard_map/ppermute | solution.py:375
  202.0 7.5 %collective-permute-done.12 = bf16[1024,512]{1,0:T(8,128)(2,1)S(1)} collective-permute-done((bf16[1024,512]{1,0:T(8,128)(2,1)S(1)}, bf16[1024,512]{1,0:T(8,128)(2,1)S(1)}, u32[]{:S(2)}, u32[]{:S(2)}) %collective-permute-start.12) | collective-permute-done | bytes 1048608 | tf_op jit(solution)/shard_map/ppermute | solution.py:362
  209.5 13.6 %collective-permute-done.15 = bf16[1024,512]{1,0:T(8,128)(2,1)S(1)} collective-permute-done((bf16[1024,512]{1,0:T(8,128)(2,1)S(1)}, bf16[1024,512]{1,0:T(8,128)(2,1)S(1)}, u32[]{:S(2)}, u32[]{:S(2)}) %collective-permute-start.15) | collective-permute-done | bytes 1048608 | tf_op jit(solution)/shard_map/ppermute | solution.py:363
  223.1 2.7 %fusion.5 = bf16[1024,512]{1,0:T(8,128)(2,1)} fusion(bf16[1024,512]{1,0:T(8,128)(2,1)S(1)} %collective-permute-done.15, bf16[1024,512]{1,0:T(8,128)(2,1)S(1)} %collective-permute-done.12, bf16[4,1024,512]{2,1,0:T(8,128)(2,1)} %collective-permute-done.9, s32[]{:T(128)S(6)} %min.22, bf16[4,1024,512]{2,1,0:T(8,128)(2,1)S(1)} %copy-done.6), kind=kLoop, calls=%fused_computation.11 | loop fusion | flops 4194304 | bytes 5242884 | tf_op jit(solution)/shard_map/convert_element_type | solution.py:388
  (57 shorter events, 19.5 us)
Async XLA Ops:
  7.2 25.7 %copy-start.8 = (s32[768]{0:T(1024)S(1)}, s32[768]{0:T(1024)}, u32[]{:S(2)}) copy-start(s32[768]{0:T(1024)} %param.11) | copy-start | bytes 9220
  7.2 75.6 %all-gather.3.cloned.1.call-start = ((), (), s32[]{:S(2)}) async-start(), calls=%async_computation | async-start | bytes 7864320 | tf_op jit(solution)/shard_map/all_gather | solution.py:334
  9.0 58.8 %copy-start.1 = (bf16[768,512]{1,0:T(8,128)(2,1)}, bf16[768,512]{1,0:T(8,128)(2,1)S(1)}, u32[]{:S(2)}) copy-start(bf16[768,512]{1,0:T(8,128)(2,1)S(1)} %constant_dynamic-update-slice_fusion.ko.vo) | copy-start | bytes 2359300
  9.0 21.7 %collective-permute-start.2 = (bf16[768,512]{1,0:T(8,128)(2,1)S(1)}, bf16[768,512]{1,0:T(8,128)(2,1)S(1)}, u32[]{:S(2)}, u32[]{:S(2)}) collective-permute-start(bf16[768,512]{1,0:T(8,128)(2,1)S(1)} %constant_dynamic-update-slice_fusion.ko.vo), channel_id=1, source_target_pairs={{0,8},{4,12},{8,16},{12,20},{16,24},{20,28},{1,9},{5,13},{9,17},{1... | collective-permute-start | bytes 2359304 | tf_op jit(solution)/shard_map/ppermute | solution.py:327
  14.0 28.8 %collective-permute-start.3 = (bf16[768,512]{1,0:T(8,128)(2,1)S(1)}, bf16[768,512]{1,0:T(8,128)(2,1)S(1)}, u32[]{:S(2)}, u32[]{:S(2)}) collective-permute-start(bf16[768,512]{1,0:T(8,128)(2,1)S(1)} %constant_dynamic-update-slice_fusion.ko.vo), channel_id=1, source_target_pairs={{0,4},{8,12},{16,20},{24,28},{1,5},{9,13},{17,21},{25,29},{2,6},{1... | collective-permute-start | bytes 2359304 | tf_op jit(solution)/shard_map/ppermute | solution.py:328
  30.7 12.1 %collective-permute-start.4 = (bf16[768,512]{1,0:T(8,128)(2,1)S(1)}, bf16[768,512]{1,0:T(8,128)(2,1)S(1)}, u32[]{:S(2)}, u32[]{:S(2)}) collective-permute-start(bf16[768,512]{1,0:T(8,128)(2,1)S(1)} %collective-permute-done.2.kd.vd), channel_id=1, source_target_pairs={{4,0},{12,8},{20,16},{28,24},{5,1},{13,9},{21,17},{29,25},{6,2},{1... | collective-permute-start | bytes 2359304 | tf_op jit(solution)/shard_map/ppermute | solution.py:329
  32.9 7.5 %collective-permute-start.1 = (s32[768]{0:T(1024)S(1)}, s32[768]{0:T(1024)S(1)}, u32[]{:S(2)}, u32[]{:S(2)}) collective-permute-start(s32[768]{0:T(1024)S(1)} %copy-done.8), channel_id=1, source_target_pairs={{0,4},{4,8},{8,12},{12,16},{16,20},{20,24},{24,28},{1,5},{5,9},{9,... | collective-permute-start | bytes 9224 | tf_op jit(solution)/shard_map/ppermute | solution.py:332
  36.0 5.7 %collective-permute-start = (s32[768]{0:T(1024)S(1)}, s32[768]{0:T(1024)S(1)}, u32[]{:S(2)}, u32[]{:S(2)}) collective-permute-start(s32[768]{0:T(1024)S(1)} %copy-done.8), channel_id=1, source_target_pairs={{0,8},{4,12},{8,16},{12,20},{16,24},{20,28},{1,9},{5,13},{9,17},{1... | collective-permute-start | bytes 9224 | tf_op jit(solution)/shard_map/ppermute | solution.py:331
  40.4 2.5 %copy-start.3 = (bf16[768,512]{1,0:T(8,128)(2,1)S(1)}, bf16[768,512]{1,0:T(8,128)(2,1)}, u32[]{:S(2)}) copy-start(bf16[768,512]{1,0:T(8,128)(2,1)} %copy-done.2) | copy-start | bytes 2359300
  67.8 22.1 %copy-start = (bf16[768,1024]{1,0:T(8,128)(2,1)}, bf16[768,1024]{1,0:T(8,128)(2,1)S(1)}, u32[]{:S(2)}) copy-start(bf16[768,1024]{1,0:T(8,128)(2,1)S(1)} %get-tuple-element.13.at_ref) | copy-start | bytes 4718596
  89.9 7.5 %collective-permute-start.9 = (bf16[4,1024,512]{2,1,0:T(8,128)(2,1)}, bf16[4,1024,512]{2,1,0:T(8,128)(2,1)}, u32[]{:S(2)}, u32[]{:S(2)}) collective-permute-start(bf16[4,1024,512]{2,1,0:T(8,128)(2,1)} %weight_blocks.3), channel_id=1, source_target_pairs={{0,4},{4,0},{8,12},{12,8},{16,20},{20,16},{24,28},{28,24},{1,5},{5... | collective-permute-start | bytes 12582920 | tf_op jit(solution)/shard_map/ppermute | solution.py:343
  101.5 26.4 %collective-permute-start.10 = (bf16[1024,512]{1,0:T(8,128)(2,1)}, bf16[1024,512]{1,0:T(8,128)(2,1)S(1)}, u32[]{:S(2)}, u32[]{:S(2)}) collective-permute-start(bf16[1024,512]{1,0:T(8,128)(2,1)} %get-tuple-element.22), channel_id=1, source_target_pairs={{0,8},{4,12},{1,9},{5,13},{2,10},{6,14},{3,11},{7,15}} | collective-permute-start | bytes 3145736 | tf_op jit(solution)/shard_map/ppermute | solution.py:362
  105.0 22.9 %copy-start.6 = (bf16[4,1024,512]{2,1,0:T(8,128)(2,1)S(1)}, bf16[4,1024,512]{2,1,0:T(8,128)(2,1)}, u32[]{:S(2)}) copy-start(bf16[4,1024,512]{2,1,0:T(8,128)(2,1)} %weight_blocks.2) | copy-start | bytes 12582916
  115.8 13.7 %copy-start.5 = (bf16[768,1024]{1,0:T(8,128)(2,1)}, bf16[768,1024]{1,0:T(8,128)(2,1)S(1)}, u32[]{:S(2)}) copy-start(bf16[768,1024]{1,0:T(8,128)(2,1)S(1)} %project_grad.1.do_ref) | copy-start | bytes 4718596
  115.8 18.3 %copy-start.4 = (bf16[768,512]{1,0:T(8,128)(2,1)S(1)}, bf16[768,512]{1,0:T(8,128)(2,1)}, u32[]{:S(2)}) copy-start(bf16[768,512]{1,0:T(8,128)(2,1)} %copy-done.2) | copy-start | bytes 2359300
  115.8 35.2 %collective-permute-start.13 = (bf16[1024,512]{1,0:T(8,128)(2,1)}, bf16[1024,512]{1,0:T(8,128)(2,1)S(1)}, u32[]{:S(2)}, u32[]{:S(2)}) collective-permute-start(bf16[1024,512]{1,0:T(8,128)(2,1)} %get-tuple-element.23), channel_id=1, source_target_pairs={{28,20},{24,16},{29,21},{25,17},{30,22},{26,18},{31,23},{27,19}} | collective-permute-start | bytes 3145736 | tf_op jit(solution)/shard_map/ppermute | solution.py:363
  129.6 26.2 %collective-permute-start.11 = (bf16[1024,512]{1,0:T(8,128)(2,1)S(1)}, bf16[1024,512]{1,0:T(8,128)(2,1)S(1)}, u32[]{:S(2)}, u32[]{:S(2)}) collective-permute-start(bf16[1024,512]{1,0:T(8,128)(2,1)S(1)} %fusion.2), channel_id=1, source_target_pairs={{0,8},{4,12},{8,16},{12,20},{1,9},{5,13},{9,17},{13,21},{2,10},{6,... | collective-permute-start | bytes 3145736 | tf_op jit(solution)/shard_map/ppermute | solution.py:362
  150.9 27.1 %collective-permute-start.5 = (bf16[768,256]{1,0:T(8,128)(2,1)S(1)}, bf16[768,256]{1,0:T(8,128)(2,1)S(1)}, u32[]{:S(2)}, u32[]{:S(2)}) collective-permute-start(bf16[768,256]{1,0:T(8,128)(2,1)S(1)} %slice.28), channel_id=1, source_target_pairs={{0,4},{4,0},{8,12},{12,8},{16,20},{20,16},{24,28},{28,24},{1,5},{5... | collective-permute-start | bytes 1179656 | tf_op jit(solution)/shard_map/ppermute | solution.py:373
  158.2 28.4 %collective-permute-start.14 = (bf16[1024,512]{1,0:T(8,128)(2,1)S(1)}, bf16[1024,512]{1,0:T(8,128)(2,1)}, u32[]{:S(2)}, u32[]{:S(2)}) collective-permute-start(bf16[1024,512]{1,0:T(8,128)(2,1)S(1)} %get-tuple-element.21), channel_id=1, source_target_pairs={{28,20},{24,16},{20,12},{16,8},{29,21},{25,17},{21,13},{17,9},{30,... | collective-permute-start | bytes 3145736 | tf_op jit(solution)/shard_map/ppermute | solution.py:363
  176.6 2.9 %collective-permute-start.7 = (bf16[768,256]{1,0:T(8,128)(2,1)S(1)}, bf16[768,256]{1,0:T(8,128)(2,1)S(1)}, u32[]{:S(2)}, u32[]{:S(2)}) collective-permute-start(bf16[768,256]{1,0:T(8,128)(2,1)S(1)} %slice.31), channel_id=1, source_target_pairs={{0,4},{4,0},{8,12},{12,8},{16,20},{20,16},{24,28},{28,24},{1,5},{5... | collective-permute-start | bytes 1179656 | tf_op jit(solution)/shard_map/ppermute | solution.py:373
  178.1 14.3 %collective-permute-start.6 = (bf16[768,256]{1,0:T(8,128)(2,1)S(1)}, bf16[768,256]{1,0:T(8,128)(2,1)S(1)}, u32[]{:S(2)}, u32[]{:S(2)}) collective-permute-start(bf16[768,256]{1,0:T(8,128)(2,1)S(1)} %fusion.12), channel_id=1, source_target_pairs={{8,0},{12,4},{16,8},{20,12},{24,16},{28,20},{9,1},{13,5},{17,9},{2... | collective-permute-start | bytes 1179656 | tf_op jit(solution)/shard_map/ppermute | solution.py:375
  179.6 21.2 %collective-permute-start.8 = (bf16[768,256]{1,0:T(8,128)(2,1)S(1)}, bf16[768,256]{1,0:T(8,128)(2,1)S(1)}, u32[]{:S(2)}, u32[]{:S(2)}) collective-permute-start(bf16[768,256]{1,0:T(8,128)(2,1)S(1)} %fusion.17), channel_id=1, source_target_pairs={{8,0},{12,4},{16,8},{20,12},{24,16},{28,20},{9,1},{13,5},{17,9},{2... | collective-permute-start | bytes 1179656 | tf_op jit(solution)/shard_map/ppermute | solution.py:375
  180.9 28.6 %collective-permute-start.12 = (bf16[1024,512]{1,0:T(8,128)(2,1)S(1)}, bf16[1024,512]{1,0:T(8,128)(2,1)S(1)}, u32[]{:S(2)}, u32[]{:S(2)}) collective-permute-start(bf16[1024,512]{1,0:T(8,128)(2,1)S(1)} %get-tuple-element.20), channel_id=1, source_target_pairs={{0,8},{4,12},{8,16},{12,20},{16,24},{20,28},{1,9},{5,13},{9,17},{1... | collective-permute-start | bytes 3145736 | tf_op jit(solution)/shard_map/ppermute | solution.py:362
  188.5 34.6 %collective-permute-start.15 = (bf16[1024,512]{1,0:T(8,128)(2,1)S(1)}, bf16[1024,512]{1,0:T(8,128)(2,1)S(1)}, u32[]{:S(2)}, u32[]{:S(2)}) collective-permute-start(bf16[1024,512]{1,0:T(8,128)(2,1)S(1)} %fusion.1), channel_id=1, source_target_pairs={{28,20},{24,16},{20,12},{16,8},{12,4},{8,0},{29,21},{25,17},{21,13... | collective-permute-start | bytes 3145736 | tf_op jit(solution)/shard_map/ppermute | solution.py:363
  (2 other events, 2.7 us)
Sparse Core Ops, SparseCore 0:
  9.9 72.8 all-gather.2
